TPU v7x, 32 devices: a whole 2x2x4 slice. The times are simulated.
32 devices in a mesh: groups: 2 (over x), mesh: 8 (over z, y), inst: 2 (over core).
Axes of the slice: x: 2, y: 2, z: 4, core: 2. Of those that a mesh axis runs over, the one named last changes fastest.
Arguments:
- observations: bfloat16 [512, 128, 128], P(('groups', 'mesh', 'inst')), parts along dimension 0, may hold values from -6 to 6
- instrument: int32 [512], P(('groups', 'mesh', 'inst')), parts along dimension 0, may hold values from 0 to 3
- routes: int32 [512, 2], P(('groups', 'mesh', 'inst')), parts along dimension 0, may hold values from 0 to 7, all different within a row; in each aligned block of 16 rows (0 to 15, 16 to 31, ...) at most 8 rows name the same one
- offsets: int32 [512, 2], P(('groups', 'mesh', 'inst')), parts along dimension 0, may hold values from 0 to 1920
- edges: bfloat16 [512, 2, 128, 128], P(('groups', 'mesh', 'inst')), parts along dimension 0, may hold values from -0.1875 to 0.1875
- w_embed: bfloat16 [4, 128, 512], replicated, may hold values from -0.5 to 0.5
- w_mix: bfloat16 [512, 512], replicated, may hold values from -0.25 to 0.25
- w_node_in: bfloat16 [512, 512], replicated, may hold values from -0.25 to 0.25
- w_node_out: bfloat16 [512, 512], replicated, may hold values from -0.25 to 0.25
Outputs:
- latents: bfloat16 [32768, 512], P(('groups', 'mesh', 'inst')), parts along dimension 0
There are 2 independent parts, one for each index of `groups`. A program takes and returns all parts, laid end to end along the dimension named above; an argument that names none is the same for every part. Nothing has to cross between parts.
Inputs may be any that keep to these rules, and one draw needn't show every extreme that they name: `routes`: each block names 2 different partitions; among the blocks of one device no partition is named more than 8 times, a bound that some block reaches.
All inputs are finite; a program needn't handle non-finite values.
Results may differ from a plain program's by a relative error of at most 0.0067.
Values may be sent and summed in bfloat16 or wider, within the bound.
A program may use at most 128 MiB of HBM per device.

v0:
```python
import functools

import jax
import jax.numpy as jnp
from jax import lax
from jax.experimental import pallas as pl
from jax.experimental.pallas import tpu as pltpu
from jax.sharding import PartitionSpec as P

NODE_PART = 2048
ANY = pl.ANY
VMEM = pltpu.VMEM
SMEM = pltpu.SMEM
MESH = pl.DeviceIdType.MESH
LIMIT = 48 * 1024 * 1024


def silu(v):
    return 0.5 * v * (1.0 + jnp.tanh(0.5 * v))


def pack_kernel(foot, source, obs, edges, out, sem):
    slots = out.shape[0]

    def step(s, carry):
        entry = source[s]
        pltpu.make_async_copy(obs.at[entry // foot], out.at[s, 0], sem).start()
        pltpu.make_async_copy(edges.at[entry], out.at[s, 1], sem).start()
        return carry

    lax.fori_loop(0, slots, step, 0)
    pltpu.make_async_copy(out, out, sem).wait()


def pack(source, obs, edges, foot):
    slots = source.shape[0]
    return pl.pallas_call(
        functools.partial(pack_kernel, foot),
        out_shape=jax.ShapeDtypeStruct((slots, 2) + obs.shape[1:], obs.dtype),
        in_specs=[
            pl.BlockSpec(memory_space=SMEM),
            pl.BlockSpec(memory_space=VMEM),
            pl.BlockSpec(memory_space=VMEM),
        ],
        out_specs=pl.BlockSpec(memory_space=ANY),
        scratch_shapes=[pltpu.SemaphoreType.DMA],
        compiler_params=pltpu.CompilerParams(vmem_limit_bytes=LIMIT),
    )(source, obs, edges)


def tiles_kernel(first_chunk, last_chunk, meta, got, w_embed, *refs):
    if first_chunk:
        out, acc = refs
        acc[...] = jnp.zeros_like(acc)
    else:
        held, out, acc = refs
        acc[:NODE_PART, :] = held[...]
    slots = got.shape[0]

    def step(s, carry):
        word = meta[s]

        @pl.when(word >= 8192)
        def _():
            kind = (word // 2048) % 4
            start = word % 2048
            v = jnp.dot(got[s, 0], w_embed[kind], preferred_element_type=jnp.float32)
            first = silu(v).astype(jnp.bfloat16)
            turn = start % 8
            base = pl.multiple_of(start - turn, 8)
            turned = pltpu.roll(got[s, 1].astype(jnp.float32), turn, 1).astype(jnp.bfloat16)
            term = lax.dot_general(
                turned, first, (((0,), (0,)), ((), ())), preferred_element_type=jnp.float32
            )
            tile_n = term.shape[0]
            head = term[:8]
            low = lax.broadcasted_iota(jnp.int32, head.shape, 0) < turn
            acc[pl.ds(base, 8), :] += jnp.where(low, 0.0, head)
            acc[pl.ds(base + 8, tile_n - 8), :] += term[8:]
            acc[pl.ds(base + tile_n, 8), :] += jnp.where(low, head, 0.0)

        return carry

    lax.fori_loop(0, slots, step, 0)
    out[...] = acc[:NODE_PART, :].astype(out.dtype)


def tiles(meta, got, w_embed, held, last_chunk):
    width = w_embed.shape[2]
    args = [meta, got, w_embed] + ([] if held is None else [held])
    return pl.pallas_call(
        functools.partial(tiles_kernel, held is None, last_chunk),
        out_shape=jax.ShapeDtypeStruct(
            (NODE_PART, width), jnp.bfloat16 if last_chunk else jnp.float32
        ),
        in_specs=[pl.BlockSpec(memory_space=SMEM)]
        + [pl.BlockSpec(memory_space=VMEM)] * (len(args) - 1),
        out_specs=pl.BlockSpec(memory_space=VMEM),
        scratch_shapes=[pltpu.VMEM((NODE_PART + 8, width), jnp.float32)],
        compiler_params=pltpu.CompilerParams(vmem_limit_bytes=LIMIT),
    )(*args)


def nodes_kernel(pieces, own_sums, w_mix, w_in, w_out, out, got, send_sem, recv_sem):
    me = lax.axis_index("inst")
    other = 1 - me
    half = out.shape[0]
    rows = half // pieces
    barrier = pltpu.get_barrier_semaphore()
    pl.semaphore_signal(barrier, inc=1, device_id={"inst": other}, device_id_type=MESH)
    pl.semaphore_wait(barrier, 1)
    copies = []
    for i in range(pieces):
        copy = pltpu.make_async_remote_copy(
            src_ref=own_sums.at[pl.ds(pl.multiple_of(other * half + i * rows, rows), rows)],
            dst_ref=got.at[pl.ds(i * rows, rows)],
            send_sem=send_sem.at[i],
            recv_sem=recv_sem.at[i],
            device_id={"inst": other},
            device_id_type=MESH,
        )
        copy.start()
        copies.append(copy)
    for i in range(pieces):
        copies[i].wait_recv()
        mine = own_sums[pl.ds(pl.multiple_of(me * half + i * rows, rows), rows), :]
        total = mine.astype(jnp.float32) + got[pl.ds(i * rows, rows), :].astype(jnp.float32)
        summed = jnp.dot(
            total.astype(jnp.bfloat16), w_mix[...], preferred_element_type=jnp.float32
        )
        scale = lax.rsqrt(jnp.mean(summed * summed, axis=1, keepdims=True) + 1e-06)
        normed = (summed * scale).astype(jnp.bfloat16)
        inner = silu(jnp.dot(normed, w_in[...], preferred_element_type=jnp.float32))
        out[pl.ds(i * rows, rows), :] = (
            summed
            + jnp.dot(inner.astype(jnp.bfloat16), w_out[...], preferred_element_type=jnp.float32)
        ).astype(out.dtype)
    for i in range(pieces):
        copies[i].wait_send()


def nodes(own_sums, w_mix, w_in, w_out, n_inst):
    total, width = own_sums.shape
    half = total // n_inst
    pieces = 4
    return pl.pallas_call(
        functools.partial(nodes_kernel, pieces),
        out_shape=jax.ShapeDtypeStruct((half, width), jnp.bfloat16),
        in_specs=[pl.BlockSpec(memory_space=VMEM)] * 4,
        out_specs=pl.BlockSpec(memory_space=VMEM),
        scratch_shapes=[
            pltpu.VMEM((half, width), jnp.bfloat16),
            pltpu.SemaphoreType.DMA((pieces,)),
            pltpu.SemaphoreType.DMA((pieces,)),
        ],
        compiler_params=pltpu.CompilerParams(
            collective_id=0, has_side_effects=True, vmem_limit_bytes=LIMIT
        ),
    )(own_sums, w_mix, w_in, w_out)


def per_device(
    observations, instrument, routes, offsets, edges, w_embed, w_mix, w_node_in, w_node_out
):
    n_mesh = lax.axis_size("mesh")
    n_inst = lax.axis_size("inst")
    blocks, obs_n, feats = observations.shape
    foot = routes.shape[1]
    tile_n = edges.shape[3]
    cap = max(2, 2 * blocks * foot // n_mesh)
    chunks = min(2, cap)
    per = cap // chunks
    slots = n_mesh * cap
    entries = blocks * foot
    dest = routes.reshape(entries)
    index = jnp.arange(entries, dtype=jnp.int32)
    same = (dest[:, None] == dest[None, :]) & (index[None, :] < index[:, None])
    rank = jnp.sum(same.astype(jnp.int32), axis=1)
    position = (rank // per) * (n_mesh * per) + dest * per + rank % per
    words = offsets.reshape(entries) + 2048 * jnp.repeat(instrument, foot) + 8192
    hit = position[None, :] == jnp.arange(slots, dtype=jnp.int32)[:, None]
    source = jnp.sum(jnp.where(hit, index[None, :], 0), axis=1)
    meta = jnp.sum(jnp.where(hit, words[None, :], 0), axis=1)
    got_meta = lax.all_to_all(
        meta.reshape(chunks, n_mesh, per), "mesh", split_axis=1, concat_axis=1, tiled=True
    ).reshape(chunks, n_mesh * per)
    packed = pack(source, observations, edges.reshape(entries, obs_n, tile_n), foot)
    packed = packed.reshape((chunks, n_mesh, per) + packed.shape[1:])
    held = None
    for k in range(chunks):
        got = lax.all_to_all(packed[k], "mesh", split_axis=0, concat_axis=0, tiled=True)
        got = got.reshape((n_mesh * per,) + got.shape[2:])
        held = tiles(got_meta[k], got, w_embed, held, k == chunks - 1)
    return nodes(held, w_mix, w_node_in, w_node_out, n_inst)


def solution(mesh):
    return jax.shard_map(
        per_device,
        mesh=mesh,
        in_specs=(
            P(("groups", "mesh", "inst"), None, None),
            P(("groups", "mesh", "inst")),
            P(("groups", "mesh", "inst"), None),
            P(("groups", "mesh", "inst"), None),
            P(("groups", "mesh", "inst"), None, None, None),
            P(),
            P(),
            P(),
            P(),
        ),
        out_specs=P(("groups", "mesh", "inst"), None),
        check_vma=False,
    )
```

profile of v0, /device:TPU:3, one launch (start us, length us, event | category | flops | bytes accessed | tf_op | source)
XLA Modules:
  0.0 145.9 jit_solution(14417893720944903345)
XLA Ops:
  0.0 0.7 broadcast_multiply_fusion
  0.7 0.7 add_add_fusion
  1.3 0.1 copy.18
  1.4 0.1 add.56
  1.5 0.8 copy.17
  2.3 0.1 eq.30
  2.4 0.2 convert_reduce_fusion
  2.6 0.1 select_reduce_fusion
  2.7 0.1 reshape.79
  2.7 0.6 copy.19
  3.4 5.6 %all-to-all-start = ((s32[2,8,4]{2,0,1:T(2,128)}), s32[2,8,4]{2,0,1:T(2,128)S(1)}, u32[]{:S(2)}, u32[]{:S(2)}) async-start(s32[2,8,4]{2,0,1:T(2,128)} %copy.19), calls=%async_computation | async-start | bytes 16384 | tf_op jit(solution)/shard_map/all_to_all | solution.py:184
  8.9 1.2 copy-done.2
  10.1 1.0 copy-done.3
  11.2 6.9 %shard_map.91 = bf16[64,2,128,128]{3,2,1,0:T(8,128)(2,1)S(1)} custom-call(s32[64]{0:T(128)S(1)} %get-tuple-element.7.source, bf16[16,128,128]{2,1,0:T(8,128)(2,1)S(1)} %copy-done.3, bf16[32,128,128]{2,1,0:T(8,128)(2,1)S(1)} %bitcast.7), custom_call_target="tpu_custom_call" | custom-call | tf_op jit(solution)/shard_map/pallas_call | solution.py:37
  18.1 1.8 %fusion.2 = (bf16[32,2,128,128]{3,2,1,0:T(8,128)(2,1)S(1)}, bf16[32,2,128,128]{3,2,1,0:T(8,128)(2,1)}) fusion(bf16[64,2,128,128]{3,2,1,0:T(8,128)(2,1)S(1)} %shard_map.91), kind=kLoop, calls=%fused_computation.16 | loop fusion | bytes 8388608 | tf_op jit(solution)/shard_map/slice | solution.py:191
  19.9 52.6 %all_to_all.15 = bf16[8,4,2,128,128]{4,3,2,1,0:T(8,128)(2,1)} all-to-all(bf16[8,4,2,128,128]{4,3,2,1,0:T(8,128)(2,1)S(1)} %bitcast.9), channel_id=1, replica_groups=mesh['groups'=2,'mesh'=8,'inst'=2] {'mesh'}, dimensions={0} | all-to-all | bytes 4194304 | tf_op jit(solution)/shard_map/all_to_all | solution.py:191
  72.5 4.2 %all-to-all-start.1 = ((bf16[8,4,2,128,128]{4,3,2,1,0:T(8,128)(2,1)}), bf16[8,4,2,128,128]{4,3,2,1,0:T(8,128)(2,1)S(1)}, u32[]{:S(2)}, u32[]{:S(2)}) async-start(bf16[8,4,2,128,128]{4,3,2,1,0:T(8,128)(2,1)} %bitcast.8), calls=%async_computation.1 | async-start | bytes 4194304 | tf_op jit(solution)/shard_map/all_to_all | solution.py:191
  76.7 0.1 squeeze.14.meta
  76.9 1.6 %copy-done = bf16[8,4,2,128,128]{4,3,2,1,0:T(8,128)(2,1)S(1)} copy-done((bf16[8,4,2,128,128]{4,3,2,1,0:T(8,128)(2,1)S(1)}, bf16[8,4,2,128,128]{4,3,2,1,0:T(8,128)(2,1)}, u32[]{:S(2)}) %copy-start) | copy-done | bytes 2097176
  78.5 14.7 %shard_map.92.refs_0_ = f32[2048,512]{1,0:T(8,128)} custom-call(s32[32]{0:T(128)S(1)} %squeeze.14.meta, bf16[32,2,128,128]{3,2,1,0:T(8,128)(2,1)S(1)} %bitcast.6, bf16[4,128,512]{2,1,0:T(8,128)(2,1)S(1)} %copy-done.1), custom_call_target="tpu_custom_call" | custom-call | tf_op jit(solution)/shard_map/pallas_call | solution.py:91
  93.2 30.3 %all-to-all-done.1 = bf16[8,4,2,128,128]{4,3,2,1,0:T(8,128)(2,1)S(1)} async-done(((bf16[8,4,2,128,128]{4,3,2,1,0:T(8,128)(2,1)}), bf16[8,4,2,128,128]{4,3,2,1,0:T(8,128)(2,1)S(1)}, u32[]{:S(2)}, u32[]{:S(2)}) %all-to-all-start.1) | async-done | bytes 2097184 | tf_op jit(solution)/shard_map/all_to_all | solution.py:191
  123.6 14.5 %shard_map.93.own_sums = bf16[2048,512]{1,0:T(8,128)(2,1)S(1)} custom-call(s32[32]{0:T(128)S(1)} %squeeze.12.meta, bf16[32,2,128,128]{3,2,1,0:T(8,128)(2,1)S(1)} %bitcast.5, bf16[4,128,512]{2,1,0:T(8,128)(2,1)S(1)} %copy-done.1, f32[2048,512]{1,0:T(8,128)} %shard_map.92.refs_0_), custom_call_target="tpu_custom_call" | custom-call | tf_op jit(solution)/shard_map/pallas_call | solution.py:91
  138.1 6.9 %shard_map.94 = bf16[1024,512]{1,0:T(8,128)(2,1)S(1)} custom-call(bf16[2048,512]{1,0:T(8,128)(2,1)S(1)} %shard_map.93.own_sums, bf16[512,512]{1,0:T(8,128)(2,1)S(1)} %copy-done.4, bf16[512,512]{1,0:T(8,128)(2,1)S(1)} %copy-done.5, bf16[512,512]{1,0:T(8,128)(2,1)S(1)} %copy-done.6), custom_call_target="tpu_custom_call" | custom-call | tf_op jit(solution)/shard_map/pallas_call | solution.py:146
  145.0 1.0 copy.21
  (15 shorter events, 0.1 us)
Async XLA Ops:
  3.4 16.5 %all-to-all-start = ((s32[2,8,4]{2,0,1:T(2,128)}), s32[2,8,4]{2,0,1:T(2,128)S(1)}, u32[]{:S(2)}, u32[]{:S(2)}) async-start(s32[2,8,4]{2,0,1:T(2,128)} %copy.19), calls=%async_computation | async-start | bytes 16384 | tf_op jit(solution)/shard_map/all_to_all | solution.py:184
  8.9 1.2 copy-start.2
  10.1 1.0 copy-start.3
  72.5 4.4 %copy-start.1 = (bf16[4,128,512]{2,1,0:T(8,128)(2,1)S(1)}, bf16[4,128,512]{2,1,0:T(8,128)(2,1)}, u32[]{:S(2)}) copy-start(bf16[4,128,512]{2,1,0:T(8,128)(2,1)} %w_embed.3) | copy-start | bytes 1572868
  72.5 51.1 %all-to-all-start.1 = ((bf16[8,4,2,128,128]{4,3,2,1,0:T(8,128)(2,1)}), bf16[8,4,2,128,128]{4,3,2,1,0:T(8,128)(2,1)S(1)}, u32[]{:S(2)}, u32[]{:S(2)}) async-start(bf16[8,4,2,128,128]{4,3,2,1,0:T(8,128)(2,1)} %bitcast.8), calls=%async_computation.1 | async-start | bytes 4194304 | tf_op jit(solution)/shard_map/all_to_all | solution.py:191
  76.9 1.6 %copy-start = (bf16[8,4,2,128,128]{4,3,2,1,0:T(8,128)(2,1)S(1)}, bf16[8,4,2,128,128]{4,3,2,1,0:T(8,128)(2,1)}, u32[]{:S(2)}) copy-start(bf16[8,4,2,128,128]{4,3,2,1,0:T(8,128)(2,1)} %all_to_all.15) | copy-start | bytes 6291460
  123.6 14.5 %copy-start.4 = (bf16[512,512]{1,0:T(8,128)(2,1)S(1)}, bf16[512,512]{1,0:T(8,128)(2,1)}, u32[]{:S(2)}) copy-start(bf16[512,512]{1,0:T(8,128)(2,1)} %w_mix.1) | copy-start | bytes 1572868
  123.6 14.5 %copy-start.5 = (bf16[512,512]{1,0:T(8,128)(2,1)S(1)}, bf16[512,512]{1,0:T(8,128)(2,1)}, u32[]{:S(2)}) copy-start(bf16[512,512]{1,0:T(8,128)(2,1)} %w_in.1) | copy-start | bytes 1572868
  123.6 14.5 %copy-start.6 = (bf16[512,512]{1,0:T(8,128)(2,1)S(1)}, bf16[512,512]{1,0:T(8,128)(2,1)}, u32[]{:S(2)}) copy-start(bf16[512,512]{1,0:T(8,128)(2,1)} %w_out.1) | copy-start | bytes 1572868
where the time goes:
time: 146 us
  blocking collectives  52.6 us (36%)
  Pallas kernels  43 us (29%)
  waiting for transfers between devices  30.3 us (21%)
  starting transfers between devices  9.76 us (7%)
  local copies, waits for them, and re-layouts  8.53 us (6%)
  other arithmetic  1.63 us (1%)
    all_to_all x1, blocking collectives, per_device(): lax.all_to_all(packed[k], 'mesh', split_axis=0, concat_axis=0, tiled=True)  52.6 us
    all_to_all x1, waiting for transfers between devices, per_device(): lax.all_to_all(packed[k], 'mesh', split_axis=0, concat_axis=0, tiled=True)  30.3 us
    pallas_call x2, Pallas kernels, tiles(): pl.pallas_call(functools.partial(tiles_kernel, held is None, last_chunk),...  29.2 us
    pallas_call x1, Pallas kernels, pack(): pl.pallas_call(functools.partial(pack_kernel, foot), out_shape=jax.ShapeD...  6.91 us
    pallas_call x1, Pallas kernels, nodes(): pl.pallas_call(functools.partial(nodes_kernel, pieces), out_shape=jax.Sha...  6.86 us
    unnamed x16, local copies, waits for them, and re-layouts  5.6 us
    all_to_all x1, starting transfers between devices, per_device(): lax.all_to_all(meta.reshape(chunks, n_mesh, per), 'mesh', split_axis=1, c...  5.55 us
    all_to_all x1, starting transfers between devices, per_device(): lax.all_to_all(packed[k], 'mesh', split_axis=0, concat_axis=0, tiled=True)  4.21 us
  transfers between devices with their start and end apart: 2, of which 1 were waited for; matrix products, arithmetic and copies ran while one was open for 1% of the time, Pallas kernels for 15%

commit v1 on v0

v1 whole, which is shorter than its diff:
```python
import functools

import jax
import jax.numpy as jnp
from jax import lax
from jax.experimental import pallas as pl
from jax.experimental.pallas import tpu as pltpu
from jax.sharding import PartitionSpec as P

NODE_PART = 2048
ANY = pl.ANY
VMEM = pltpu.VMEM
SMEM = pltpu.SMEM
MESH = pl.DeviceIdType.MESH
LIMIT = 48 * 1024 * 1024


def silu(v):
    return 0.5 * v * (1.0 + jnp.tanh(0.5 * v))


def pack_kernel(foot, source, meta, obs, edges, out):
    tile_n = edges.shape[2]

    def step(s, carry):
        entry = source[s]
        out[s, 0] = obs[entry // foot]
        nodes_first = edges[entry].astype(jnp.float32).T
        out[s, 1] = pltpu.roll(nodes_first, meta[s] % tile_n, 0).astype(out.dtype)
        return carry

    lax.fori_loop(0, out.shape[0], step, 0)


def pack(source, meta, obs, edges, foot):
    slots = source.shape[0]
    return pl.pallas_call(
        functools.partial(pack_kernel, foot),
        out_shape=jax.ShapeDtypeStruct((slots, 2) + obs.shape[1:], obs.dtype),
        in_specs=[pl.BlockSpec(memory_space=SMEM)] * 2 + [pl.BlockSpec(memory_space=VMEM)] * 2,
        out_specs=pl.BlockSpec(memory_space=VMEM),
        compiler_params=pltpu.CompilerParams(vmem_limit_bytes=LIMIT),
    )(source, meta, obs, edges)


def main_kernel(
    packed, words, w_embed, w_mix, w_in, w_out, out,
    got, got_words, acc, kinds_obs, first, placed, leaving, arrived,
    send_sem, recv_sem, word_send, word_recv, half_send, half_recv,
):
    cap, n_mesh = got.shape[0], got.shape[1]
    tile_n, feats = got.shape[3], got.shape[4]
    n_kinds = w_embed.shape[0] // feats
    unit = kinds_obs.shape[0] // tile_n
    groups = n_mesh // unit
    half = out.shape[0]
    pieces = half_send.shape[0]
    rows = half // pieces
    me = lax.axis_index("mesh")
    core = lax.axis_index("inst")
    other = 1 - core

    barrier = pltpu.get_barrier_semaphore()

    def greet(i, carry):
        to = lax.rem(me + i, n_mesh)
        pl.semaphore_signal(barrier, inc=1, device_id={"mesh": to}, device_id_type=MESH)
        return carry

    lax.fori_loop(1, n_mesh, greet, 0)
    pl.semaphore_signal(barrier, inc=1, device_id={"inst": other}, device_id_type=MESH)

    def own(j):
        return pltpu.make_async_copy(packed.at[j, me], got.at[j, me], recv_sem.at[j, me])

    def own_words():
        return pltpu.make_async_copy(words.at[me], got_words.at[me], word_recv.at[me])

    def start_own(j, carry):
        own(j).start()
        return carry

    own_words().start()
    lax.fori_loop(0, cap, start_own, 0)
    acc[...] = jnp.zeros_like(acc)
    pl.semaphore_wait(barrier, n_mesh)

    def entry_copy(j, to):
        return pltpu.make_async_remote_copy(
            src_ref=packed.at[j, to],
            dst_ref=got.at[j, me],
            send_sem=send_sem.at[j, to],
            recv_sem=recv_sem.at[j, me],
            device_id={"mesh": to},
            device_id_type=MESH,
        )

    def word_copy(to):
        return pltpu.make_async_remote_copy(
            src_ref=words.at[to],
            dst_ref=got_words.at[me],
            send_sem=word_send.at[to],
            recv_sem=word_recv.at[me],
            device_id={"mesh": to},
            device_id_type=MESH,
        )

    def start_words(i, carry):
        word_copy(lax.rem(me + i, n_mesh)).start()
        return carry

    lax.fori_loop(1, n_mesh, start_words, 0)

    def start_rank(j, carry):
        def start_one(i, c):
            entry_copy(j, lax.rem(me + i, n_mesh)).start()
            return c

        return lax.fori_loop(1, n_mesh, start_one, carry)

    lax.fori_loop(0, cap, start_rank, 0)

    def wait_words(s, carry):
        pltpu.make_async_copy(words.at[s], got_words.at[s], word_recv.at[s]).wait()
        return carry

    lax.fori_loop(0, n_mesh, wait_words, 0)

    place = lax.broadcasted_iota(jnp.int32, (tile_n, tile_n), 0)
    group_rows = placed.shape[0]
    tiles = group_rows // tile_n

    def work(u, carry):
        j = u // groups
        base = (u % groups) * unit
        owners = []
        for s in range(unit):
            src = base + s
            pltpu.make_async_copy(packed.at[j, src], got.at[j, src], recv_sem.at[j, src]).wait()
            word = got_words[src, pl.ds(j, 1), :]
            kind = (word // NODE_PART) % 4
            x = got[j, src, 0]
            for k in range(n_kinds):
                mask = jnp.broadcast_to((kind == k).astype(jnp.float32), (tile_n, feats))
                kinds_obs[s * tile_n : (s + 1) * tile_n, k * feats : (k + 1) * feats] = (
                    x * mask.astype(jnp.bfloat16)
                )
            begin = word % NODE_PART
            q = jnp.where(word >= 4 * NODE_PART, begin // tile_n, -100)
            owner = q + jnp.where(place < begin % tile_n, 1, 0)
            owners.append(owner.astype(jnp.float32).astype(jnp.bfloat16))
        first[...] = silu(
            jnp.dot(kinds_obs[...], w_embed[...], preferred_element_type=jnp.float32)
        ).astype(jnp.bfloat16)
        for g in range(NODE_PART // group_rows):
            for s in range(unit):
                weights = got[j, base + s, 1]
                for n in range(tiles):
                    here = owners[s] == jnp.bfloat16(g * tiles + n)
                    placed[n * tile_n : (n + 1) * tile_n, s * tile_n : (s + 1) * tile_n] = (
                        jnp.where(here, weights, jnp.bfloat16(0))
                    )
            acc[g * group_rows : (g + 1) * group_rows, :] += jnp.dot(
                placed[...], first[...], preferred_element_type=jnp.float32
            )
        return carry

    lax.fori_loop(0, cap * groups, work, 0)

    def half_copy(i):
        return pltpu.make_async_remote_copy(
            src_ref=leaving.at[pl.ds(i * rows, rows)],
            dst_ref=arrived.at[pl.ds(i * rows, rows)],
            send_sem=half_send.at[i],
            recv_sem=half_recv.at[i],
            device_id={"inst": other},
            device_id_type=MESH,
        )

    for i in range(pieces):
        theirs = acc[pl.ds(pl.multiple_of(other * half + i * rows, rows), rows), :]
        leaving[pl.ds(i * rows, rows), :] = theirs.astype(jnp.bfloat16)
        half_copy(i).start()
    for i in range(pieces):
        half_copy(i).wait_recv()
        mine = acc[pl.ds(pl.multiple_of(core * half + i * rows, rows), rows), :]
        total = mine + arrived[pl.ds(i * rows, rows), :].astype(jnp.float32)
        summed = jnp.dot(
            total.astype(jnp.bfloat16), w_mix[...], preferred_element_type=jnp.float32
        )
        scale = lax.rsqrt(jnp.mean(summed * summed, axis=1, keepdims=True) + 1e-06)
        normed = (summed * scale).astype(jnp.bfloat16)
        inner = silu(jnp.dot(normed, w_in[...], preferred_element_type=jnp.float32))
        out[pl.ds(i * rows, rows), :] = (
            summed
            + jnp.dot(inner.astype(jnp.bfloat16), w_out[...], preferred_element_type=jnp.float32)
        ).astype(out.dtype)
    for i in range(pieces):
        half_copy(i).wait_send()

    def end_rank(j, carry):
        def end_one(i, c):
            entry_copy(j, lax.rem(me + i, n_mesh)).wait_send()
            return c

        return lax.fori_loop(1, n_mesh, end_one, carry)

    def end_words(i, carry):
        word_copy(lax.rem(me + i, n_mesh)).wait_send()
        return carry

    lax.fori_loop(0, cap, end_rank, 0)
    lax.fori_loop(1, n_mesh, end_words, 0)


def main(packed, words, w_embed, w_mix, w_in, w_out, n_inst):
    cap, n_mesh, _, obs_n, feats = packed.shape
    width = w_mix.shape[0]
    half = NODE_PART // n_inst
    unit = min(8, n_mesh)
    pieces = 4
    bf16 = jnp.bfloat16
    return pl.pallas_call(
        main_kernel,
        out_shape=jax.ShapeDtypeStruct((half, width), bf16),
        in_specs=[pl.BlockSpec(memory_space=VMEM)] * 6,
        out_specs=pl.BlockSpec(memory_space=VMEM),
        scratch_shapes=[
            pltpu.VMEM(packed.shape, bf16),
            pltpu.VMEM(words.shape, jnp.int32),
            pltpu.VMEM((NODE_PART, width), jnp.float32),
            pltpu.VMEM((unit * obs_n, w_embed.shape[0]), bf16),
            pltpu.VMEM((unit * obs_n, width), bf16),
            pltpu.VMEM((512, unit * obs_n), bf16),
            pltpu.VMEM((half, width), bf16),
            pltpu.VMEM((half, width), bf16),
            pltpu.SemaphoreType.DMA((cap, n_mesh)),
            pltpu.SemaphoreType.DMA((cap, n_mesh)),
            pltpu.SemaphoreType.DMA((n_mesh,)),
            pltpu.SemaphoreType.DMA((n_mesh,)),
            pltpu.SemaphoreType.DMA((pieces,)),
            pltpu.SemaphoreType.DMA((pieces,)),
        ],
        compiler_params=pltpu.CompilerParams(
            collective_id=0, has_side_effects=True, vmem_limit_bytes=LIMIT
        ),
    )(packed, words, w_embed, w_mix, w_in, w_out)


def per_device(
    observations, instrument, routes, offsets, edges, w_embed, w_mix, w_node_in, w_node_out
):
    n_mesh = lax.axis_size("mesh")
    n_inst = lax.axis_size("inst")
    blocks, obs_n, feats = observations.shape
    foot = routes.shape[1]
    tile_n = edges.shape[3]
    cap = max(2, 2 * blocks * foot // n_mesh)
    slots = n_mesh * cap
    entries = blocks * foot
    dest = routes.reshape(entries)
    index = jnp.arange(entries, dtype=jnp.int32)
    same = (dest[:, None] == dest[None, :]) & (index[None, :] < index[:, None])
    rank = jnp.sum(same.astype(jnp.int32), axis=1)
    position = rank * n_mesh + dest
    words = offsets.reshape(entries) + NODE_PART * jnp.repeat(instrument, foot) + 4 * NODE_PART
    hit = position[None, :] == jnp.arange(slots, dtype=jnp.int32)[:, None]
    source = jnp.sum(jnp.where(hit, index[None, :], 0), axis=1)
    meta = jnp.sum(jnp.where(hit, words[None, :], 0), axis=1)
    packed = pack(source, meta, observations, edges.reshape(entries, obs_n, tile_n), foot)
    packed = packed.reshape((cap, n_mesh) + packed.shape[1:])
    by_dest = jnp.pad(meta.reshape(cap, n_mesh).T, ((0, 0), (0, max(8, cap) - cap)))
    spread = jnp.broadcast_to(by_dest[:, :, None], by_dest.shape + (feats,))
    return main(
        packed, spread, w_embed.reshape(-1, w_embed.shape[2]), w_mix, w_node_in, w_node_out, n_inst
    )


def solution(mesh):
    return jax.shard_map(
        per_device,
        mesh=mesh,
        in_specs=(
            P(("groups", "mesh", "inst"), None, None),
            P(("groups", "mesh", "inst")),
            P(("groups", "mesh", "inst"), None),
            P(("groups", "mesh", "inst"), None),
            P(("groups", "mesh", "inst"), None, None, None),
            P(),
            P(),
            P(),
            P(),
        ),
        out_specs=P(("groups", "mesh", "inst"), None),
        check_vma=False,
    )
```

time: 146 us -> 124 us (0.85)
  the two profiles are of different devices: /device:TPU:3 before, /device:TPU:15 now
where the time goes in v1:
time: 124 us
  Pallas kernels  116 us (94%)
  local copies, waits for them, and re-layouts  6.43 us (5%)
  other arithmetic  1.62 us (1%)
    pallas_call x1, Pallas kernels, main(): pl.pallas_call(main_kernel, out_shape=jax.ShapeDtypeStruct((half, width),...  108 us
    pallas_call x1, Pallas kernels, pack(): pl.pallas_call(functools.partial(pack_kernel, foot), out_shape=jax.ShapeD...  7.72 us
    unnamed x16, local copies, waits for them, and re-layouts  5.95 us

profile of v1, /device:TPU:15, one launch (start us, length us, event | category | flops | bytes accessed | tf_op | source)
XLA Modules:
  0.0 123.9 jit_solution(10002150204861490668)
XLA Ops:
  0.0 0.7 broadcast_multiply_fusion
  0.7 0.7 add_add_fusion
  1.3 0.1 copy.17
  1.4 0.1 add.32
  1.5 0.8 copy.16
  2.3 0.1 eq.28
  2.4 0.2 convert_reduce_fusion
  2.6 0.1 select_reduce_fusion
  2.7 0.1 reshape.44
  2.7 0.1 copy.18
  2.8 0.1 broadcast_in_dim.37.words
  2.9 0.0 copy-start.1
  2.9 1.2 copy-done.1
  4.1 0.0 copy-start.6
  4.1 1.0 copy-done.6
  5.2 7.7 %shard_map.91 = bf16[64,2,128,128]{3,2,1,0:T(8,128)(2,1)S(1)} custom-call(s32[64]{0:T(128)S(1)} %get-tuple-element.6.source, s32[64]{0:T(128)S(1)} %get-tuple-element.5.meta, bf16[16,128,128]{2,1,0:T(8,128)(2,1)S(1)} %copy-done.6, bf16[32,128,128]{2,1,0:T(8,128)(2,1)S(1)} %bitcast.5), custom_call_target="tpu_custom_call" | custom-call | tf_op jit(solution)/shard_map/pallas_call | solution.py:37
  12.9 0.0 copy-start
  12.9 1.9 %copy-done = bf16[64,2,128,128]{3,2,1,0:T(8,128)(2,1)} copy-done((bf16[64,2,128,128]{3,2,1,0:T(8,128)(2,1)}, bf16[64,2,128,128]{3,2,1,0:T(8,128)(2,1)S(1)}, u32[]{:S(2)}) %copy-start) | copy-done | bytes 4194328
  14.8 0.0 copy-done.2
  14.8 0.0 copy-done.3
  14.8 0.0 copy-done.4
  14.8 0.0 copy-done.5
  14.8 108.1 %shard_map.92 = bf16[1024,512]{1,0:T(8,128)(2,1)S(1)} custom-call(bf16[8,8,2,128,128]{4,3,2,1,0:T(8,128)(2,1)} %bitcast.4, s32[8,8,128]{2,1,0:T(8,128)S(1)} %broadcast_in_dim.37.words, bf16[512,512]{1,0:T(8,128)(2,1)S(1)} %bitcast.6, bf16[512,512]{1,0:T(8,128)(2,1)S(1)} %copy-done.3, bf16[512,512]{1,0:T(8,128)(2,1)S(1)} %copy-done.4, ...), custom_call_target="tpu_custom_call" | custom-call | tf_op jit(solution)/shard_map/pallas_call | solution.py:223
  122.9 1.0 copy.20
  (5 shorter events, 0.0 us)
Async XLA Ops:
  2.9 1.2 %copy-start.1 = (bf16[16,2,128,128]{3,2,1,0:T(8,128)(2,1)S(1)}, bf16[16,2,128,128]{3,2,1,0:T(8,128)(2,1)}, u32[]{:S(2)}) copy-start(bf16[16,2,128,128]{3,2,1,0:T(8,128)(2,1)} %param.13) | copy-start | bytes 3145732
  4.1 1.0 copy-start.6
  5.2 9.7 %copy-start.2 = (bf16[4,128,512]{2,1,0:T(8,128)(2,1)S(1)}, bf16[4,128,512]{2,1,0:T(8,128)(2,1)}, u32[]{:S(2)}) copy-start(bf16[4,128,512]{2,1,0:T(8,128)(2,1)} %param.14) | copy-start | bytes 1572868
  5.2 9.7 %copy-start.3 = (bf16[512,512]{1,0:T(8,128)(2,1)S(1)}, bf16[512,512]{1,0:T(8,128)(2,1)}, u32[]{:S(2)}) copy-start(bf16[512,512]{1,0:T(8,128)(2,1)} %w_mix.1) | copy-start | bytes 1572868
  5.2 9.7 %copy-start.4 = (bf16[512,512]{1,0:T(8,128)(2,1)S(1)}, bf16[512,512]{1,0:T(8,128)(2,1)}, u32[]{:S(2)}) copy-start(bf16[512,512]{1,0:T(8,128)(2,1)} %w_in.1) | copy-start | bytes 1572868
  5.2 9.7 %copy-start.5 = (bf16[512,512]{1,0:T(8,128)(2,1)S(1)}, bf16[512,512]{1,0:T(8,128)(2,1)}, u32[]{:S(2)}) copy-start(bf16[512,512]{1,0:T(8,128)(2,1)} %w_out.1) | copy-start | bytes 1572868
  12.9 1.9 %copy-start = (bf16[64,2,128,128]{3,2,1,0:T(8,128)(2,1)}, bf16[64,2,128,128]{3,2,1,0:T(8,128)(2,1)S(1)}, u32[]{:S(2)}) copy-start(bf16[64,2,128,128]{3,2,1,0:T(8,128)(2,1)S(1)} %shard_map.91) | copy-start | bytes 12582916

commit v2 on v1

v2 whole, which is shorter than its diff:
```python
import functools

import jax
import jax.numpy as jnp
from jax import lax
from jax.experimental import pallas as pl
from jax.experimental.pallas import tpu as pltpu
from jax.sharding import PartitionSpec as P

NODE_PART = 2048
ANY = pl.ANY
VMEM = pltpu.VMEM
SMEM = pltpu.SMEM
MESH = pl.DeviceIdType.MESH
LIMIT = 48 * 1024 * 1024
RELAY = True


def silu(v):
    return 0.5 * v * (1.0 + jnp.tanh(0.5 * v))


def main_kernel(
    relay, foot, source, obs, edges, words, w_embed, w_mix, w_in, w_out, out,
    packed, got, got_words, acc, kinds_obs, first, placed, leaving, arrived,
    far_leaving, far_arrived, dense_out, dense_in,
    send_sem, recv_sem, word_send, word_recv, half_send, half_recv,
    far_send, far_recv, dense_send, dense_recv,
):
    parts, cap, n_part = got.shape[0], got.shape[1], got.shape[2]
    n_mesh = parts * n_part
    tile_n, feats = got.shape[4], got.shape[5]
    n_kinds = w_embed.shape[0] // feats
    unit = kinds_obs.shape[0] // tile_n
    half = out.shape[0]
    pieces = half_send.shape[0]
    rows = half // pieces
    me = lax.axis_index("mesh")
    part = me // n_part
    place_in = lax.rem(me, n_part)
    across = lax.rem(me + n_part, n_mesh)
    core = lax.axis_index("inst")
    other = 1 - core

    def device(k):
        return part * n_part + k

    def dest(f, k):
        return lax.rem(part + parts - 1 - f, parts) * n_part + k

    barrier = pltpu.get_barrier_semaphore()

    def greet(t, carry):
        to = device(lax.rem(place_in + t, n_part))
        pl.semaphore_signal(barrier, inc=1, device_id={"mesh": to}, device_id_type=MESH)
        return carry

    lax.fori_loop(1, n_part, greet, 0)
    if relay:
        pl.semaphore_signal(barrier, inc=1, device_id={"mesh": across}, device_id_type=MESH)
    pl.semaphore_signal(barrier, inc=1, device_id={"inst": other}, device_id_type=MESH)

    def pack(f, j):
        def one(k, carry):
            entry = source[j * n_mesh + dest(f, k)]
            packed[f, j, k, 0] = obs[entry // foot]
            packed[f, j, k, 1] = edges[entry]
            return carry

        lax.fori_loop(0, n_part, one, 0)

    def entry_copy(f, j, k):
        return pltpu.make_async_remote_copy(
            src_ref=packed.at[f, j, k],
            dst_ref=got.at[f, j, place_in],
            send_sem=send_sem.at[f, j, k],
            recv_sem=recv_sem.at[f, j, place_in],
            device_id={"mesh": device(k)},
            device_id_type=MESH,
        )

    def word_copy(f, k):
        return pltpu.make_async_remote_copy(
            src_ref=words.at[dest(f, k)],
            dst_ref=got_words.at[f, place_in],
            send_sem=word_send.at[f, k],
            recv_sem=word_recv.at[f, place_in],
            device_id={"mesh": device(k)},
            device_id_type=MESH,
        )

    pack(0, 0)
    pl.semaphore_wait(barrier, n_part + (1 if relay else 0))
    for f in range(parts):
        pltpu.make_async_copy(
            words.at[dest(f, place_in)], got_words.at[f, place_in], word_recv.at[f, place_in]
        ).start()

        def start_word(t, carry):
            word_copy(f, lax.rem(place_in + t, n_part)).start()
            return carry

        lax.fori_loop(1, n_part, start_word, 0)

    for f in range(parts):

        def start_rank(j, carry):
            if f == 0:

                @pl.when(j > 0)
                def _():
                    pack(f, j)

            else:
                pack(f, j)
            pltpu.make_async_copy(
                packed.at[f, j, place_in], got.at[f, j, place_in], recv_sem.at[f, j, place_in]
            ).start()

            def start_one(t, c):
                entry_copy(f, j, lax.rem(place_in + t, n_part)).start()
                return c

            return lax.fori_loop(1, n_part, start_one, carry)

        lax.fori_loop(0, cap, start_rank, 0)

    for f in range(parts):

        def wait_word(s, carry):
            pltpu.make_async_copy(words.at[s], got_words.at[f, s], word_recv.at[f, s]).wait()
            return carry

        lax.fori_loop(0, n_part, wait_word, 0)

    place = lax.broadcasted_iota(jnp.int32, (tile_n, tile_n), 0)
    lane = lax.broadcasted_iota(jnp.int32, (tile_n, tile_n), 1)
    group_rows = placed.shape[0]
    tiles = group_rows // tile_n

    def sums(f):
        acc[...] = jnp.zeros_like(acc)

        def work(u, carry):
            owners = []
            turned = []
            for s in range(unit):
                slot = u * unit + s
                j = slot // n_part
                src = lax.rem(slot, n_part)
                pltpu.make_async_copy(
                    packed.at[f, j, src], got.at[f, j, src], recv_sem.at[f, j, src]
                ).wait()
                word = got_words[f, src, pl.ds(j, 1), :]
                kind = (word // NODE_PART) % 4
                x = got[f, j, src, 0]
                for k in range(n_kinds):
                    mask = jnp.broadcast_to((kind == k).astype(jnp.float32), (tile_n, feats))
                    kinds_obs[s * tile_n : (s + 1) * tile_n, k * feats : (k + 1) * feats] = (
                        x * mask.astype(jnp.bfloat16)
                    )
                begin = word % NODE_PART
                turn = begin % tile_n
                q = jnp.where(word >= 4 * NODE_PART, begin // tile_n, -100)
                owner = q + jnp.where(place < turn, 1, 0)
                owners.append(owner.astype(jnp.float32).astype(jnp.bfloat16))
                moves = jnp.where((lane + turn) % tile_n == place, 1.0, 0.0).astype(jnp.bfloat16)
                turned.append(
                    lax.dot_general(
                        moves, got[f, j, src, 1], (((1,), (1,)), ((), ())),
                        preferred_element_type=jnp.float32,
                    ).astype(jnp.bfloat16)
                )
            first[...] = silu(
                jnp.dot(kinds_obs[...], w_embed[...], preferred_element_type=jnp.float32)
            ).astype(jnp.bfloat16)
            for g in range(NODE_PART // group_rows):
                for s in range(unit):
                    for n in range(tiles):
                        here = owners[s] == jnp.bfloat16(g * tiles + n)
                        placed[n * tile_n : (n + 1) * tile_n, s * tile_n : (s + 1) * tile_n] = (
                            jnp.where(here, turned[s], jnp.bfloat16(0))
                        )
                acc[g * group_rows : (g + 1) * group_rows, :] += jnp.dot(
                    placed[...], first[...], preferred_element_type=jnp.float32
                )
            return carry

        lax.fori_loop(0, cap * n_part // unit, work, 0)

    def to_core(src, dst, sent, come, i):
        return pltpu.make_async_remote_copy(
            src_ref=src.at[pl.ds(i * rows, rows)],
            dst_ref=dst.at[pl.ds(i * rows, rows)],
            send_sem=sent.at[i],
            recv_sem=come.at[i],
            device_id={"inst": other},
            device_id_type=MESH,
        )

    def far_copy(i):
        return to_core(far_leaving, far_arrived, far_send, far_recv, i)

    def half_copy(i):
        return to_core(leaving, arrived, half_send, half_recv, i)

    def dense_copy(i):
        return pltpu.make_async_remote_copy(
            src_ref=dense_out.at[pl.ds(i * rows, rows)],
            dst_ref=dense_in.at[pl.ds(i * rows, rows)],
            send_sem=dense_send.at[i],
            recv_sem=dense_recv.at[i],
            device_id={"mesh": across},
            device_id_type=MESH,
        )

    def theirs(i):
        return acc[pl.ds(pl.multiple_of(other * half + i * rows, rows), rows), :]

    def ours(i):
        return acc[pl.ds(pl.multiple_of(core * half + i * rows, rows), rows), :]

    sums(0)
    if relay:
        for i in range(pieces):
            far_leaving[pl.ds(i * rows, rows), :] = theirs(i).astype(jnp.bfloat16)
            far_copy(i).start()
        for i in range(pieces):
            far_copy(i).wait_recv()
            dense_out[pl.ds(i * rows, rows), :] = (
                ours(i) + far_arrived[pl.ds(i * rows, rows), :].astype(jnp.float32)
            ).astype(jnp.bfloat16)
            dense_copy(i).start()
        sums(1)
    for i in range(pieces):
        leaving[pl.ds(i * rows, rows), :] = theirs(i).astype(jnp.bfloat16)
        half_copy(i).start()
    for i in range(pieces):
        half_copy(i).wait_recv()
        total = ours(i) + arrived[pl.ds(i * rows, rows), :].astype(jnp.float32)
        if relay:
            dense_copy(i).wait_recv()
            total += dense_in[pl.ds(i * rows, rows), :].astype(jnp.float32)
        summed = jnp.dot(
            total.astype(jnp.bfloat16), w_mix[...], preferred_element_type=jnp.float32
        )
        scale = lax.rsqrt(jnp.mean(summed * summed, axis=1, keepdims=True) + 1e-06)
        normed = (summed * scale).astype(jnp.bfloat16)
        inner = silu(jnp.dot(normed, w_in[...], preferred_element_type=jnp.float32))
        out[pl.ds(i * rows, rows), :] = (
            summed
            + jnp.dot(inner.astype(jnp.bfloat16), w_out[...], preferred_element_type=jnp.float32)
        ).astype(out.dtype)
    for i in range(pieces):
        half_copy(i).wait_send()
        if relay:
            far_copy(i).wait_send()
            dense_copy(i).wait_send()
    for f in range(parts):

        def end_rank(j, carry):
            def end_one(t, c):
                entry_copy(f, j, lax.rem(place_in + t, n_part)).wait_send()
                return c

            return lax.fori_loop(1, n_part, end_one, carry)

        def end_word(t, carry):
            word_copy(f, lax.rem(place_in + t, n_part)).wait_send()
            return carry

        lax.fori_loop(0, cap, end_rank, 0)
        lax.fori_loop(1, n_part, end_word, 0)


def main(relay, foot, cap, source, obs, edges, words, w_embed, w_mix, w_in, w_out, n_inst):
    n_mesh = words.shape[0]
    _, obs_n, feats = obs.shape
    width = w_mix.shape[0]
    half = NODE_PART // n_inst
    parts = 2 if relay else 1
    n_part = n_mesh // parts
    unit = min(8, cap * n_part)
    pieces = 4
    bf16 = jnp.bfloat16
    entry = (2, obs_n, feats)
    half_rows = pltpu.VMEM((half, width), bf16)
    return pl.pallas_call(
        functools.partial(main_kernel, relay, foot),
        out_shape=jax.ShapeDtypeStruct((half, width), bf16),
        in_specs=[pl.BlockSpec(memory_space=SMEM)] + [pl.BlockSpec(memory_space=VMEM)] * 7,
        out_specs=pl.BlockSpec(memory_space=VMEM),
        scratch_shapes=[
            pltpu.VMEM((parts, cap, n_part) + entry, bf16),
            pltpu.VMEM((parts, cap, n_part) + entry, bf16),
            pltpu.VMEM((parts, n_part) + words.shape[1:], jnp.int32),
            pltpu.VMEM((NODE_PART, width), jnp.float32),
            pltpu.VMEM((unit * obs_n, w_embed.shape[0]), bf16),
            pltpu.VMEM((unit * obs_n, width), bf16),
            pltpu.VMEM((512, unit * obs_n), bf16),
        ]
        + [half_rows] * 6
        + [pltpu.SemaphoreType.DMA((parts, cap, n_part))] * 2
        + [pltpu.SemaphoreType.DMA((parts, n_part))] * 2
        + [pltpu.SemaphoreType.DMA((pieces,))] * 6,
        compiler_params=pltpu.CompilerParams(
            collective_id=0, has_side_effects=True, vmem_limit_bytes=LIMIT
        ),
    )(source, obs, edges, words, w_embed, w_mix, w_in, w_out)


def per_device(
    observations, instrument, routes, offsets, edges, w_embed, w_mix, w_node_in, w_node_out
):
    n_mesh = lax.axis_size("mesh")
    n_inst = lax.axis_size("inst")
    blocks, obs_n, feats = observations.shape
    foot = routes.shape[1]
    tile_n = edges.shape[3]
    cap = max(2, 2 * blocks * foot // n_mesh)
    slots = n_mesh * cap
    entries = blocks * foot
    dest = routes.reshape(entries)
    index = jnp.arange(entries, dtype=jnp.int32)
    same = (dest[:, None] == dest[None, :]) & (index[None, :] < index[:, None])
    rank = jnp.sum(same.astype(jnp.int32), axis=1)
    position = rank * n_mesh + dest
    words = offsets.reshape(entries) + NODE_PART * jnp.repeat(instrument, foot) + 4 * NODE_PART
    hit = position[None, :] == jnp.arange(slots, dtype=jnp.int32)[:, None]
    source = jnp.sum(jnp.where(hit, index[None, :], 0), axis=1)
    meta = jnp.sum(jnp.where(hit, words[None, :], 0), axis=1)
    by_dest = jnp.pad(meta.reshape(cap, n_mesh).T, ((0, 0), (0, max(8, cap) - cap)))
    spread = jnp.broadcast_to(by_dest[:, :, None], by_dest.shape + (feats,))
    return main(
        RELAY, foot, cap, source, observations, edges.reshape(entries, obs_n, tile_n), spread,
        w_embed.reshape(-1, w_embed.shape[2]), w_mix, w_node_in, w_node_out, n_inst,
    )


def solution(mesh):
    return jax.shard_map(
        per_device,
        mesh=mesh,
        in_specs=(
            P(("groups", "mesh", "inst"), None, None),
            P(("groups", "mesh", "inst")),
            P(("groups", "mesh", "inst"), None),
            P(("groups", "mesh", "inst"), None),
            P(("groups", "mesh", "inst"), None, None, None),
            P(),
            P(),
            P(),
            P(),
        ),
        out_specs=P(("groups", "mesh", "inst"), None),
        check_vma=False,
    )
```

time: 124 us -> 95.8 us (0.77)
  the two profiles are of different devices: /device:TPU:15 before, /device:TPU:3 now
where the time goes in v2:
time: 95.8 us; the launch traced here: 94.6 us
  Pallas kernels  84.3 us (88%)
  local copies, waits for them, and re-layouts  9.91 us (10%)
    pallas_call x1, Pallas kernels, main(): pl.pallas_call(functools.partial(main_kernel, relay, foot), out_shape=jax...  84.3 us
    unnamed x20, local copies, waits for them, and re-layouts  9.42 us

profile of v2, /device:TPU:3, one launch (start us, length us, event | category | flops | bytes accessed | tf_op | source)
XLA Modules:
  0.0 94.6 jit_solution(6016432209371112968)
XLA Ops:
  0.0 0.0 copy-start.8
  0.0 0.7 copy-done.8
  0.7 0.0 copy-start.7
  0.7 0.7 copy-done.7
  1.3 0.1 copy.17
  1.4 0.0 copy-start.6
  1.4 0.1 add.32
  1.5 0.6 copy-done.6
  2.1 0.1 copy.16
  2.2 0.1 eq.28
  2.3 0.2 convert_reduce_fusion
  2.5 0.1 select_reduce_fusion
  2.6 0.1 reshape.40
  2.6 0.1 copy.18
  2.7 0.1 broadcast_in_dim.37.words
  2.8 0.0 copy-start
  2.8 1.2 %copy-done = bf16[16,2,128,128]{3,2,1,0:T(8,128)(2,1)S(1)} copy-done((bf16[16,2,128,128]{3,2,1,0:T(8,128)(2,1)S(1)}, bf16[16,2,128,128]{3,2,1,0:T(8,128)(2,1)}, u32[]{:S(2)}) %copy-start) | copy-done | bytes 1048600
  4.0 1.0 %copy-done.1 = bf16[16,128,128]{2,1,0:T(8,128)(2,1)S(1)} copy-done((bf16[16,128,128]{2,1,0:T(8,128)(2,1)S(1)}, bf16[16,128,128]{2,1,0:T(8,128)(2,1)}, u32[]{:S(2)}) %copy-start.1) | copy-done | bytes 524312
  5.1 1.0 %copy-done.2 = bf16[4,128,512]{2,1,0:T(8,128)(2,1)S(1)} copy-done((bf16[4,128,512]{2,1,0:T(8,128)(2,1)S(1)}, bf16[4,128,512]{2,1,0:T(8,128)(2,1)}, u32[]{:S(2)}) %copy-start.2) | copy-done | bytes 524312
  6.1 1.0 %copy-done.3 = bf16[512,512]{1,0:T(8,128)(2,1)S(1)} copy-done((bf16[512,512]{1,0:T(8,128)(2,1)S(1)}, bf16[512,512]{1,0:T(8,128)(2,1)}, u32[]{:S(2)}) %copy-start.3) | copy-done | bytes 524312
  7.2 1.0 %copy-done.4 = bf16[512,512]{1,0:T(8,128)(2,1)S(1)} copy-done((bf16[512,512]{1,0:T(8,128)(2,1)S(1)}, bf16[512,512]{1,0:T(8,128)(2,1)}, u32[]{:S(2)}) %copy-start.4) | copy-done | bytes 524312
  8.2 1.0 %copy-done.5 = bf16[512,512]{1,0:T(8,128)(2,1)S(1)} copy-done((bf16[512,512]{1,0:T(8,128)(2,1)S(1)}, bf16[512,512]{1,0:T(8,128)(2,1)}, u32[]{:S(2)}) %copy-start.5) | copy-done | bytes 524312
  9.2 84.3 %shard_map.91 = bf16[1024,512]{1,0:T(8,128)(2,1)S(1)} custom-call(s32[64]{0:T(128)S(1)} %get-tuple-element.6.source, bf16[16,128,128]{2,1,0:T(8,128)(2,1)S(1)} %copy-done.1, bf16[32,128,128]{2,1,0:T(8,128)(2,1)S(1)} %bitcast.3, s32[8,8,128]{2,1,0:T(8,128)S(1)} %broadcast_in_dim.37.words, bf16[512,512]{1,0:T(8,128)(2,1)S(1)} %bitcast.4, ...), custom_call_target="tpu_custom_call" | custom-call | tf_op jit(solution)/shard_map/pallas_call | solution.py:288
  93.6 1.0 %copy.20 = bf16[1024,512]{1,0:T(8,128)(2,1)} copy(bf16[1024,512]{1,0:T(8,128)(2,1)S(1)} %shard_map.91) | data formatting | bytes 2097152
  (8 shorter events, 0.0 us)
Async XLA Ops:
  0.0 0.7 copy-start.8
  0.7 0.7 copy-start.7
  1.4 0.7 copy-start.6
  2.8 1.2 %copy-start = (bf16[16,2,128,128]{3,2,1,0:T(8,128)(2,1)S(1)}, bf16[16,2,128,128]{3,2,1,0:T(8,128)(2,1)}, u32[]{:S(2)}) copy-start(bf16[16,2,128,128]{3,2,1,0:T(8,128)(2,1)} %param.13) | copy-start | bytes 3145732
  4.0 1.0 %copy-start.1 = (bf16[16,128,128]{2,1,0:T(8,128)(2,1)S(1)}, bf16[16,128,128]{2,1,0:T(8,128)(2,1)}, u32[]{:S(2)}) copy-start(bf16[16,128,128]{2,1,0:T(8,128)(2,1)} %obs.1) | copy-start | bytes 1572868
  5.1 1.0 %copy-start.2 = (bf16[4,128,512]{2,1,0:T(8,128)(2,1)S(1)}, bf16[4,128,512]{2,1,0:T(8,128)(2,1)}, u32[]{:S(2)}) copy-start(bf16[4,128,512]{2,1,0:T(8,128)(2,1)} %param.14) | copy-start | bytes 1572868
  6.1 1.0 %copy-start.3 = (bf16[512,512]{1,0:T(8,128)(2,1)S(1)}, bf16[512,512]{1,0:T(8,128)(2,1)}, u32[]{:S(2)}) copy-start(bf16[512,512]{1,0:T(8,128)(2,1)} %w_mix.1) | copy-start | bytes 1572868
  7.2 1.0 %copy-start.4 = (bf16[512,512]{1,0:T(8,128)(2,1)S(1)}, bf16[512,512]{1,0:T(8,128)(2,1)}, u32[]{:S(2)}) copy-start(bf16[512,512]{1,0:T(8,128)(2,1)} %w_in.1) | copy-start | bytes 1572868
  8.2 1.0 %copy-start.5 = (bf16[512,512]{1,0:T(8,128)(2,1)S(1)}, bf16[512,512]{1,0:T(8,128)(2,1)}, u32[]{:S(2)}) copy-start(bf16[512,512]{1,0:T(8,128)(2,1)} %w_out.1) | copy-start | bytes 1572868

commit v3 on v2

--- a/solution.py
+++ b/solution.py
@@ -12,7 +12,7 @@
 VMEM = pltpu.VMEM
 SMEM = pltpu.SMEM
 MESH = pl.DeviceIdType.MESH
-LIMIT = 48 * 1024 * 1024
+LIMIT = 58 * 1024 * 1024
 RELAY = True
 
 
@@ -21,8 +21,8 @@
 
 
 def main_kernel(
-    relay, foot, source, obs, edges, words, w_embed, w_mix, w_in, w_out, out,
-    packed, got, got_words, acc, kinds_obs, first, placed, leaving, arrived,
+    relay, foot, source, obs_at, edges_at, words, w_embed_at, w_mix_at, w_in_at, w_out_at, out,
+    obs, edges, w_embed, w_mix, w_in, w_out, load_sem, packed, got, got_words, acc, kinds_obs, first, placed, leaving, arrived,
     far_leaving, far_arrived, dense_out, dense_in,
     send_sem, recv_sem, word_send, word_recv, half_send, half_recv,
     far_send, far_recv, dense_send, dense_recv,
@@ -48,6 +48,16 @@
     def dest(f, k):
         return lax.rem(part + parts - 1 - f, parts) * n_part + k
 
+    loads = [
+        pltpu.make_async_copy(src, dst, load_sem.at[i])
+        for i, (src, dst) in enumerate(
+            [(obs_at, obs), (edges_at, edges), (w_embed_at, w_embed), (w_mix_at, w_mix),
+             (w_in_at, w_in), (w_out_at, w_out)]
+        )
+    ]
+    for load in loads:
+        load.start()
+
     barrier = pltpu.get_barrier_semaphore()
 
     def greet(t, carry):
@@ -89,6 +99,8 @@
             device_id_type=MESH,
         )
 
+    loads[0].wait()
+    loads[1].wait()
     pack(0, 0)
     pl.semaphore_wait(barrier, n_part + (1 if relay else 0))
     for f in range(parts):
@@ -220,6 +232,8 @@
     def ours(i):
         return acc[pl.ds(pl.multiple_of(core * half + i * rows, rows), rows), :]
 
+    for load in loads[2:]:
+        load.wait()
     sums(0)
     if relay:
         for i in range(pieces):
@@ -235,6 +249,21 @@
     for i in range(pieces):
         leaving[pl.ds(i * rows, rows), :] = theirs(i).astype(jnp.bfloat16)
         half_copy(i).start()
+    for f in range(parts):
+
+        def end_rank(j, carry):
+            def end_one(t, c):
+                entry_copy(f, j, lax.rem(place_in + t, n_part)).wait_send()
+                return c
+
+            return lax.fori_loop(1, n_part, end_one, carry)
+
+        def end_word(t, carry):
+            word_copy(f, lax.rem(place_in + t, n_part)).wait_send()
+            return carry
+
+        lax.fori_loop(0, cap, end_rank, 0)
+        lax.fori_loop(1, n_part, end_word, 0)
     for i in range(pieces):
         half_copy(i).wait_recv()
         total = ours(i) + arrived[pl.ds(i * rows, rows), :].astype(jnp.float32)
@@ -256,21 +285,6 @@
         if relay:
             far_copy(i).wait_send()
             dense_copy(i).wait_send()
-    for f in range(parts):
-
-        def end_rank(j, carry):
-            def end_one(t, c):
-                entry_copy(f, j, lax.rem(place_in + t, n_part)).wait_send()
-                return c
-
-            return lax.fori_loop(1, n_part, end_one, carry)
-
-        def end_word(t, carry):
-            word_copy(f, lax.rem(place_in + t, n_part)).wait_send()
-            return carry
-
-        lax.fori_loop(0, cap, end_rank, 0)
-        lax.fori_loop(1, n_part, end_word, 0)
 
 
 def main(relay, foot, cap, source, obs, edges, words, w_embed, w_mix, w_in, w_out, n_inst):
@@ -280,17 +294,22 @@
     half = NODE_PART // n_inst
     parts = 2 if relay else 1
     n_part = n_mesh // parts
-    unit = min(8, cap * n_part)
-    pieces = 4
+    unit = min(4, cap * n_part)
+    pieces = 8
     bf16 = jnp.bfloat16
     entry = (2, obs_n, feats)
     half_rows = pltpu.VMEM((half, width), bf16)
     return pl.pallas_call(
         functools.partial(main_kernel, relay, foot),
         out_shape=jax.ShapeDtypeStruct((half, width), bf16),
-        in_specs=[pl.BlockSpec(memory_space=SMEM)] + [pl.BlockSpec(memory_space=VMEM)] * 7,
+        in_specs=[pl.BlockSpec(memory_space=SMEM)]
+        + [pl.BlockSpec(memory_space=ANY)] * 2
+        + [pl.BlockSpec(memory_space=VMEM)]
+        + [pl.BlockSpec(memory_space=ANY)] * 4,
         out_specs=pl.BlockSpec(memory_space=VMEM),
-        scratch_shapes=[
+        scratch_shapes=[pltpu.VMEM(a.shape, bf16) for a in (obs, edges, w_embed, w_mix, w_in, w_out)]
+        + [
+            pltpu.SemaphoreType.DMA((6,)),
             pltpu.VMEM((parts, cap, n_part) + entry, bf16),
             pltpu.VMEM((parts, cap, n_part) + entry, bf16),
             pltpu.VMEM((parts, n_part) + words.shape[1:], jnp.int32),

time: 95.8 us -> 91.3 us (0.953)
  local copies, waits for them, and re-layouts: 9.91 us -> 5.37 us
    unnamed x20 -> x8, local copies, waits for them, and re-layouts: 9.42 us -> 4.27 us
where the time goes in v3:
time: 91.3 us; the launch traced here: 90.1 us
  Pallas kernels  83.8 us (92%)
  local copies, waits for them, and re-layouts  5.37 us (6%)
    pallas_call x1, Pallas kernels, main(): pl.pallas_call(functools.partial(main_kernel, relay, foot), out_shape=jax...  83.8 us
    unnamed x8, local copies, waits for them, and re-layouts  4.27 us

profile of v3, /device:TPU:3, one launch (start us, length us, event | category | flops | bytes accessed | tf_op | source)
XLA Modules:
  0.0 90.1 jit_solution(2920388417563613793)
XLA Ops:
  0.0 0.0 copy-start.2
  0.0 0.7 copy-done.2
  0.7 0.0 copy-start.1
  0.7 0.7 copy-done.1
  1.3 0.1 copy.17
  1.4 0.0 copy-start
  1.4 0.1 add.32
  1.5 0.6 copy-done
  2.1 0.1 copy.16
  2.2 0.1 eq.28
  2.3 0.2 convert_reduce_fusion
  2.5 0.7 select_reduce_fusion
  3.2 0.1 reshape.40
  3.2 0.1 copy.18
  3.3 0.7 broadcast_in_dim.37.words
  4.0 83.8 %shard_map.91 = bf16[1024,512]{1,0:T(8,128)(2,1)} custom-call(s32[64]{0:T(128)} %get-tuple-element.6.source, bf16[16,128,128]{2,1,0:T(8,128)(2,1)} %obs_at.1, bf16[32,128,128]{2,1,0:T(8,128)(2,1)} %bitcast.3, s32[8,8,128]{2,1,0:T(8,128)} %broadcast_in_dim.37.words, bf16[512,512]{1,0:T(8,128)(2,1)} %bitcast.4, bf16[512,512]{1,0:T(8,128)(2,1)} %w_mix_at.1, ...), custom_call_target="tpu_custom_call" | custom-call | tf_op jit(solution)/shard_map/pallas_call | solution.py:302
  87.8 2.3 %copy.20 = bf16[1024,512]{1,0:T(8,128)(2,1)} copy(bf16[1024,512]{1,0:T(8,128)(2,1)} %shard_map.91) | data formatting | bytes 2097152
  (3 shorter events, 0.0 us)
Async XLA Ops:
  0.0 0.7 copy-start.2
  0.7 0.7 copy-start.1
  1.4 0.7 copy-start

commit v4 on v3

--- a/solution.py
+++ b/solution.py
@@ -12,7 +12,7 @@
 VMEM = pltpu.VMEM
 SMEM = pltpu.SMEM
 MESH = pl.DeviceIdType.MESH
-LIMIT = 58 * 1024 * 1024
+LIMIT = 48 * 1024 * 1024
 RELAY = True
 
 

time: 91.3 us -> 94.2 us (1.032)
  local copies, waits for them, and re-layouts: 5.37 us -> 9.91 us
  Pallas kernels: 83.8 us -> 82.6 us
    unnamed x8 -> x20, local copies, waits for them, and re-layouts: 4.27 us -> 9.42 us
    pallas_call x1, Pallas kernels: 83.8 us -> 82.6 us  [main(): pl.pallas_call(functools.partial(main_kernel, relay, foot), out_shape=jax...]
where the time goes in v4:
time: 94.2 us; the launch traced here: 92.8 us
  Pallas kernels  82.6 us (88%)
  local copies, waits for them, and re-layouts  9.91 us (11%)
    pallas_call x1, Pallas kernels, main(): pl.pallas_call(functools.partial(main_kernel, relay, foot), out_shape=jax...  82.6 us
    unnamed x20, local copies, waits for them, and re-layouts  9.42 us

profile of v4, /device:TPU:3, one launch (start us, length us, event | category | flops | bytes accessed | tf_op | source)
XLA Modules:
  0.0 92.8 jit_solution(1216164314999419910)
XLA Ops:
  0.0 0.0 copy-start.8
  0.0 0.7 copy-done.8
  0.7 0.0 copy-start.7
  0.7 0.7 copy-done.7
  1.3 0.1 copy.17
  1.4 0.0 copy-start.6
  1.4 0.1 add.32
  1.5 0.6 copy-done.6
  2.1 0.1 copy.16
  2.2 0.1 eq.28
  2.3 0.2 convert_reduce_fusion
  2.5 0.1 select_reduce_fusion
  2.6 0.1 reshape.40
  2.6 0.1 copy.18
  2.7 0.1 broadcast_in_dim.37.words
  2.8 0.0 copy-start
  2.8 1.2 %copy-done = bf16[16,2,128,128]{3,2,1,0:T(8,128)(2,1)S(1)} copy-done((bf16[16,2,128,128]{3,2,1,0:T(8,128)(2,1)S(1)}, bf16[16,2,128,128]{3,2,1,0:T(8,128)(2,1)}, u32[]{:S(2)}) %copy-start) | copy-done | bytes 1048600
  4.0 1.0 %copy-done.1 = bf16[16,128,128]{2,1,0:T(8,128)(2,1)S(1)} copy-done((bf16[16,128,128]{2,1,0:T(8,128)(2,1)S(1)}, bf16[16,128,128]{2,1,0:T(8,128)(2,1)}, u32[]{:S(2)}) %copy-start.1) | copy-done | bytes 524312
  5.1 1.0 %copy-done.2 = bf16[4,128,512]{2,1,0:T(8,128)(2,1)S(1)} copy-done((bf16[4,128,512]{2,1,0:T(8,128)(2,1)S(1)}, bf16[4,128,512]{2,1,0:T(8,128)(2,1)}, u32[]{:S(2)}) %copy-start.2) | copy-done | bytes 524312
  6.1 1.0 %copy-done.3 = bf16[512,512]{1,0:T(8,128)(2,1)S(1)} copy-done((bf16[512,512]{1,0:T(8,128)(2,1)S(1)}, bf16[512,512]{1,0:T(8,128)(2,1)}, u32[]{:S(2)}) %copy-start.3) | copy-done | bytes 524312
  7.2 1.0 %copy-done.4 = bf16[512,512]{1,0:T(8,128)(2,1)S(1)} copy-done((bf16[512,512]{1,0:T(8,128)(2,1)S(1)}, bf16[512,512]{1,0:T(8,128)(2,1)}, u32[]{:S(2)}) %copy-start.4) | copy-done | bytes 524312
  8.2 1.0 %copy-done.5 = bf16[512,512]{1,0:T(8,128)(2,1)S(1)} copy-done((bf16[512,512]{1,0:T(8,128)(2,1)S(1)}, bf16[512,512]{1,0:T(8,128)(2,1)}, u32[]{:S(2)}) %copy-start.5) | copy-done | bytes 524312
  9.2 82.6 %shard_map.91 = bf16[1024,512]{1,0:T(8,128)(2,1)S(1)} custom-call(s32[64]{0:T(128)S(1)} %get-tuple-element.6.source, bf16[16,128,128]{2,1,0:T(8,128)(2,1)S(1)} %copy-done.1, bf16[32,128,128]{2,1,0:T(8,128)(2,1)S(1)} %bitcast.3, s32[8,8,128]{2,1,0:T(8,128)S(1)} %broadcast_in_dim.37.words, bf16[512,512]{1,0:T(8,128)(2,1)S(1)} %bitcast.4, ...), custom_call_target="tpu_custom_call" | custom-call | tf_op jit(solution)/shard_map/pallas_call | solution.py:302
  91.8 1.0 %copy.20 = bf16[1024,512]{1,0:T(8,128)(2,1)} copy(bf16[1024,512]{1,0:T(8,128)(2,1)S(1)} %shard_map.91) | data formatting | bytes 2097152
  (8 shorter events, 0.0 us)
Async XLA Ops:
  0.0 0.7 copy-start.8
  0.7 0.7 copy-start.7
  1.4 0.7 copy-start.6
  2.8 1.2 %copy-start = (bf16[16,2,128,128]{3,2,1,0:T(8,128)(2,1)S(1)}, bf16[16,2,128,128]{3,2,1,0:T(8,128)(2,1)}, u32[]{:S(2)}) copy-start(bf16[16,2,128,128]{3,2,1,0:T(8,128)(2,1)} %param.13) | copy-start | bytes 3145732
  4.0 1.0 %copy-start.1 = (bf16[16,128,128]{2,1,0:T(8,128)(2,1)S(1)}, bf16[16,128,128]{2,1,0:T(8,128)(2,1)}, u32[]{:S(2)}) copy-start(bf16[16,128,128]{2,1,0:T(8,128)(2,1)} %obs_at.1) | copy-start | bytes 1572868
  5.1 1.0 %copy-start.2 = (bf16[4,128,512]{2,1,0:T(8,128)(2,1)S(1)}, bf16[4,128,512]{2,1,0:T(8,128)(2,1)}, u32[]{:S(2)}) copy-start(bf16[4,128,512]{2,1,0:T(8,128)(2,1)} %param.14) | copy-start | bytes 1572868
  6.1 1.0 %copy-start.3 = (bf16[512,512]{1,0:T(8,128)(2,1)S(1)}, bf16[512,512]{1,0:T(8,128)(2,1)}, u32[]{:S(2)}) copy-start(bf16[512,512]{1,0:T(8,128)(2,1)} %w_mix_at.1) | copy-start | bytes 1572868
  7.2 1.0 %copy-start.4 = (bf16[512,512]{1,0:T(8,128)(2,1)S(1)}, bf16[512,512]{1,0:T(8,128)(2,1)}, u32[]{:S(2)}) copy-start(bf16[512,512]{1,0:T(8,128)(2,1)} %w_in_at.1) | copy-start | bytes 1572868
  8.2 1.0 %copy-start.5 = (bf16[512,512]{1,0:T(8,128)(2,1)S(1)}, bf16[512,512]{1,0:T(8,128)(2,1)}, u32[]{:S(2)}) copy-start(bf16[512,512]{1,0:T(8,128)(2,1)} %w_out_at.1) | copy-start | bytes 1572868
